TPU v7x, 512 devices: a whole 4x4x16 slice. The times are simulated.
512 devices in a mesh: section: 16 (over y, x), tm: 32 (over z, core).
Axes of the slice: x: 4, y: 4, z: 16, core: 2. Of those that a mesh axis runs over, the one named last changes fastest.
Arguments:
- series: bfloat16 [7, 4096, 1024], P(None, 'tm', 'section'), may hold values from -6 to 6
- query_key_value_weight: bfloat16 [16, 1024, 1536], P('section'), may hold values from -1.25 to 1.25, as said below
- output_weight: bfloat16 [16, 512, 1024], P('section'), may hold values from -0.25 to 0.25
- gain: float32 [16, 1024], P('section'), may hold values from 0.5 to 1.5
- readout_weight: float32 [16, 1024], P('section'), may hold values from -0.046875 to 0.046875
- dilation_block: int32 [64], replicated, may hold values from 0 to 1
- order: int32 [7], replicated, may hold values from 0 to 6, each once
Outputs:
- rul: float32 [7, 32, 128], P(None, 'tm', 'section')
Inputs may be any that keep to these rules, and one draw needn't show every extreme that they name: `query_key_value_weight`: entries of order the inverse square root of 1024. `order`: A permutation of the slots.
All inputs are finite; a program needn't handle non-finite values.
Results may differ from a plain program's by a relative error of at most 0.025.
Values may be sent and summed in bfloat16 or wider, within the bound.
A program may use at most 64 MiB of HBM per device.

v0:
```python
import jax
import jax.numpy as jnp
from jax import lax
from jax.sharding import PartitionSpec as P

HEADS_L = 4
HEADS_D = 4
HD = 64
WINDOW = 256
BLK = 64


EPSILON = 1e-05


def from_behind(value, axis, steps):
    count = lax.axis_size(axis)
    leading, last = (max(0, -steps), min(count, count - steps))
    return lax.ppermute(value, axis, [(source, source + steps) for source in range(leading, last)])


def passed_along(value, axis, steps):
    count = lax.axis_size(axis)
    pairs = [(source, (source + steps) % count) for source in range(count)]
    return lax.ppermute(value, axis, pairs)


def norm_rows(values):
    return values * lax.rsqrt(jnp.mean(values * values, axis=-1, keepdims=True) + EPSILON)


def soft_weights(scores, allowed):
    if allowed is not None:
        scores = jnp.where(allowed, scores, -1e30)
    top_score = jnp.max(scores, axis=-1, keepdims=True)
    raised = jnp.exp(scores - top_score)
    return (raised / jnp.sum(raised, axis=-1, keepdims=True)).astype(jnp.bfloat16)


def local(
    series, query_key_value_weight, output_weight, gain, readout_weight, dilation_block, order
):
    section_id = lax.axis_index("section")
    section_count = lax.axis_size("section")
    my_shard = lax.axis_index("tm")
    shard_count = lax.axis_size("tm")
    half_away = shard_count // 2
    micro_count = series.shape[0]
    row_count = series.shape[1]
    model_width = query_key_value_weight.shape[1]
    weight_qkv = query_key_value_weight[0]
    weight_out = output_weight[0]
    norm_gain = gain[0]
    read_vector = readout_weight[0]
    local_width = HEADS_L * HD
    dilated_width = HEADS_D * HD
    head_width = local_width + dilated_width
    block_total = row_count // BLK
    score_scale = HD ** (-0.5)
    highest = lax.Precision.HIGHEST
    tick_count = micro_count + section_count - 1
    span_count = max(1, WINDOW // row_count)
    wanted_shard = (my_shard + half_away) % shard_count
    wanted_blocks = lax.dynamic_slice_in_dim(
        dilation_block, wanted_shard * block_total, block_total, 0
    )
    query_pos = my_shard * row_count + jnp.arange(row_count, dtype=jnp.int32)
    key_pos = my_shard * row_count - WINDOW + jnp.arange(WINDOW + row_count, dtype=jnp.int32)
    window_mask = (
        (key_pos[None, :] > query_pos[:, None] - WINDOW)
        & (key_pos[None, :] <= query_pos[:, None])
        & (key_pos[None, :] >= 0)
    )

    def project(hidden):
        normed = (norm_rows(hidden.astype(jnp.float32)) * norm_gain).astype(jnp.bfloat16)
        return jnp.dot(normed, weight_qkv, preferred_element_type=jnp.float32)

    def skip_project(hidden):
        return jnp.zeros((row_count, 3 * head_width), jnp.float32)

    def attend(operands):
        hidden, projected, window_kv, far_kv = operands
        query_cols = projected[:, :head_width]
        key_cols = projected[:, head_width : 2 * head_width]
        value_cols = projected[:, 2 * head_width :]
        near_keys = jnp.concatenate(
            [window_kv[:, :local_width], key_cols[:, :local_width]], axis=0
        ).reshape(WINDOW + row_count, HEADS_L, HD)
        near_values = jnp.concatenate(
            [window_kv[:, local_width:], value_cols[:, :local_width]], axis=0
        ).reshape(WINDOW + row_count, HEADS_L, HD)
        near_queries = query_cols[:, :local_width].reshape(row_count, HEADS_L, HD)
        near_scores = (
            jnp.einsum("qhd,khd->hqk", near_queries, near_keys, precision=highest) * score_scale
        )
        near_weights = soft_weights(near_scores, window_mask[None])
        near_out = jnp.einsum(
            "hqk,khd->qhd", near_weights.astype(jnp.float32), near_values, precision=highest
        ).reshape(row_count, local_width)
        far_queries = query_cols[:, local_width:].reshape(block_total, BLK, HEADS_D, HD)
        own_keys = key_cols[:, local_width:].reshape(block_total, BLK, HEADS_D, HD)
        own_values = value_cols[:, local_width:].reshape(block_total, BLK, HEADS_D, HD)
        far_all = far_kv.reshape(block_total, BLK, 2 * dilated_width)
        far_keys = jnp.concatenate(
            [own_keys, far_all[:, :, :dilated_width].reshape(block_total, BLK, HEADS_D, HD)], axis=1
        )
        far_values = jnp.concatenate(
            [own_values, far_all[:, :, dilated_width:].reshape(block_total, BLK, HEADS_D, HD)],
            axis=1,
        )
        far_scores = (
            jnp.einsum("nqhd,nkhd->nhqk", far_queries, far_keys, precision=highest) * score_scale
        )
        far_weights = soft_weights(far_scores, None)
        far_out = jnp.einsum(
            "nhqk,nkhd->nqhd", far_weights.astype(jnp.float32), far_values, precision=highest
        ).reshape(row_count, dilated_width)
        heads_out = jnp.concatenate([near_out, far_out], axis=1).astype(jnp.bfloat16)
        updated = (
            hidden.astype(jnp.float32)
            + jnp.dot(heads_out, weight_out, preferred_element_type=jnp.float32)
        ).astype(jnp.bfloat16)
        readout = jnp.sum(norm_rows(updated.astype(jnp.float32)) * read_vector, axis=1)
        return (updated, readout)

    def skip_attend(operands):
        return (operands[0], jnp.zeros((row_count,), jnp.float32))

    def run_tick(tick_index, incoming_state, totals, first_input):
        slot_index = tick_index - section_id
        active = (slot_index >= 0) & (slot_index < micro_count)
        clipped = jnp.clip(slot_index, 0, micro_count - 1)
        hidden = jnp.where(section_id == 0, first_input, incoming_state)
        projected = lax.cond(active, project, skip_project, hidden)
        local_kv = jnp.concatenate(
            [
                projected[:, head_width : head_width + local_width],
                projected[:, 2 * head_width : 2 * head_width + local_width],
            ],
            axis=1,
        )
        pieces = []
        for distance in range(1, span_count + 1):
            pieces.append(from_behind(local_kv, "tm", distance))
        window_kv = jnp.concatenate(pieces[::-1], axis=0)
        far_local = jnp.concatenate(
            [
                projected[:, head_width + local_width : 2 * head_width],
                projected[:, 2 * head_width + local_width :],
            ],
            axis=1,
        )
        outgoing = far_local.reshape(block_total, BLK, 2 * dilated_width)[wanted_blocks].reshape(
            row_count, 2 * dilated_width
        )
        far_kv = passed_along(outgoing, "tm", half_away)
        updated, readout = lax.cond(
            active, attend, skip_attend, (hidden, projected, window_kv, far_kv)
        )
        picker = (jnp.arange(micro_count, dtype=jnp.int32) == clipped).astype(jnp.float32)
        totals = totals + picker[:, None] * readout[None, :]
        passed_on = from_behind(updated, "section", 1)
        return (passed_on, totals)

    initial = (
        jnp.zeros((row_count, model_width), jnp.bfloat16),
        jnp.zeros((micro_count, row_count), jnp.float32),
    )
    whole_series = lax.all_gather(series, "section", axis=2, tiled=True)

    def tick_all(tick_index, carry):
        slot_here = jnp.clip(tick_index, 0, micro_count - 1)
        picked = lax.dynamic_index_in_dim(order, slot_here, 0, keepdims=False)
        first_input = lax.dynamic_index_in_dim(whole_series, picked, 0, keepdims=False)
        return run_tick(tick_index, carry[0], carry[1], first_input)

    final_state, totals = lax.fori_loop(0, tick_count, tick_all, initial)
    shares = lax.psum_scatter(totals, "section", scatter_dimension=1, tiled=True)
    return shares.reshape(micro_count, 1, row_count // section_count)


def solution(mesh):
    placed = (
        P(None, "tm", "section"),
        P("section", None, None),
        P("section", None, None),
        P("section", None),
        P("section", None),
        P(),
        P(),
    )
    return jax.shard_map(
        local, mesh=mesh, in_specs=placed, out_specs=P(None, "tm", "section"), check_vma=False
    )
```

profile of v0, /device:TPU:1, one launch (start us, length us, event | category | flops | bytes accessed | tf_op | source)
XLA Modules:
  0.0 1558.0 jit_solution(16294063501692997884)
XLA Ops:
  11.2 63.0 %all-gather.2.cloned.1.call-done = bf16[7,128,1024]{1,2,0:T(8,128)(2,1)} async-done(((bf16[7,128,64]{1,2,0:T(8,128)(2,1)}), bf16[7,128,1024]{1,2,0:T(8,128)(2,1)}) %all-gather.2.cloned.1.call-update) | async-done | bytes 1835024 | tf_op jit(solution)/shard_map/all_gather | solution.py:170
  74.3 1345.6 %while.17 = (s32[]{:T(128)}, bf16[128,1024]{1,0:T(8,128)(2,1)S(1)}, f32[7,128]{1,0:T(8,128)S(1)}, s32[]{:T(128)}, pred[]{:T(512)}, /*index=5*/s32[7]{0:T(128)}, ...) while((s32[]{:T(128)}, bf16[128,1024]{1,0:T(8,128)(2,1)S(1)}, ...), condition=%wide.region_12.13_spmd.clone, body=%wide.region_0.12_spmd.clone.sunk | while | flops 944509184 | bytes 34627248 | solution.py:178
  103.2 25.3 %collective-permute-done.2 = f32[128,512]{1,0:T(8,128)S(1)} collective-permute-done((f32[128,512]{1,0:T(8,128)S(1)}, f32[128,512]{1,0:T(8,128)S(1)}, u32[]{:S(2)}, u32[]{:S(2)}) %collective-permute-start.2) | collective-permute-done | bytes 262176 | tf_op jit(solution)/shard_map/while/body/eval_jaxpr/ppermute | solution.py:25
  168.4 14.2 collective-permute-done.2
  182.6 10.6 conditional.7
  210.2 20.1 %collective-permute-start.1 = (f32[128,512]{0,1:T(8,128)S(1)}, f32[128,512]{0,1:T(8,128)}, u32[]{:S(2)}, u32[]{:S(2)}) collective-permute-start(f32[128,512]{0,1:T(8,128)S(1)} %pad_maximum_fusion.8), channel_id=1, source_target_pairs={{0,2},{1,3},{2,4},{3,5},{4,6},{5,7},{6,8},{7,9},{8,10},{9,11},{10,... | collective-permute-start | bytes 786440 | tf_op jit(solution)/shard_map/while/body/eval_jaxpr/ppermute | solution.py:19
  303.8 11.3 collective-permute-done.1
  316.2 11.2 collective-permute-done.2
  379.7 11.4 collective-permute-done.2
  439.6 12.0 collective-permute-done.2
  503.1 12.3 collective-permute-done.2
  542.9 10.6 collective-permute-start.1
  577.8 16.7 %collective-permute-start.3 = (bf16[128,1024]{1,0:T(8,128)(2,1)S(1)}, bf16[128,1024]{1,0:T(8,128)(2,1)S(1)}, u32[]{:S(2)}, u32[]{:S(2)}) collective-permute-start(bf16[128,1024]{1,0:T(8,128)(2,1)S(1)} %get-tuple-element.576), channel_id=1, source_target_pairs={{0,32},{32,64},{64,96},{96,128},{128,160},{160,192},{192,224},{224... | collective-permute-start | bytes 786440 | tf_op jit(solution)/shard_map/while/body/eval_jaxpr/ppermute | solution.py:19
  607.6 12.4 collective-permute-start.1
  650.6 18.5 %collective-permute-start = (f32[128,512]{0,1:T(8,128)S(1)}, f32[128,512]{0,1:T(8,128)}, u32[]{:S(2)}, u32[]{:S(2)}) collective-permute-start(f32[128,512]{0,1:T(8,128)S(1)} %pad_maximum_fusion.8), channel_id=1, source_target_pairs={{0,1},{1,2},{2,3},{3,4},{4,5},{5,6},{6,7},{7,8},{8,9},{9,10},{10,1... | collective-permute-start | bytes 786440 | tf_op jit(solution)/shard_map/while/body/eval_jaxpr/ppermute | solution.py:19
  699.7 16.4 %collective-permute-start.3 = (bf16[128,1024]{1,0:T(8,128)(2,1)S(1)}, bf16[128,1024]{1,0:T(8,128)(2,1)S(1)}, u32[]{:S(2)}, u32[]{:S(2)}) collective-permute-start(bf16[128,1024]{1,0:T(8,128)(2,1)S(1)} %get-tuple-element.576), channel_id=1, source_target_pairs={{0,32},{32,64},{64,96},{96,128},{128,160},{160,192},{192,224},{224... | collective-permute-start | bytes 786440 | tf_op jit(solution)/shard_map/while/body/eval_jaxpr/ppermute | solution.py:19
  729.0 12.7 collective-permute-start.1
  775.4 12.3 collective-permute-start
  820.3 15.7 %collective-permute-start.3 = (bf16[128,1024]{1,0:T(8,128)(2,1)S(1)}, bf16[128,1024]{1,0:T(8,128)(2,1)S(1)}, u32[]{:S(2)}, u32[]{:S(2)}) collective-permute-start(bf16[128,1024]{1,0:T(8,128)(2,1)S(1)} %get-tuple-element.576), channel_id=1, source_target_pairs={{0,32},{32,64},{64,96},{96,128},{128,160},{160,192},{192,224},{224... | collective-permute-start | bytes 786440 | tf_op jit(solution)/shard_map/while/body/eval_jaxpr/ppermute | solution.py:19
  925.7 12.2 collective-permute-done.2
  938.5 17.7 %collective-permute-start.3 = (bf16[128,1024]{1,0:T(8,128)(2,1)S(1)}, bf16[128,1024]{1,0:T(8,128)(2,1)S(1)}, u32[]{:S(2)}, u32[]{:S(2)}) collective-permute-start(bf16[128,1024]{1,0:T(8,128)(2,1)S(1)} %get-tuple-element.576), channel_id=1, source_target_pairs={{0,32},{32,64},{64,96},{96,128},{128,160},{160,192},{192,224},{224... | collective-permute-start | bytes 786440 | tf_op jit(solution)/shard_map/while/body/eval_jaxpr/ppermute | solution.py:19
  1057.8 12.7 collective-permute-start.3
  1084.0 12.2 collective-permute-start.1
  1104.7 11.0 collective-permute-done.2
  1116.3 16.0 %collective-permute-start.3 = (bf16[128,1024]{1,0:T(8,128)(2,1)S(1)}, bf16[128,1024]{1,0:T(8,128)(2,1)S(1)}, u32[]{:S(2)}, u32[]{:S(2)}) collective-permute-start(bf16[128,1024]{1,0:T(8,128)(2,1)S(1)} %get-tuple-element.576), channel_id=1, source_target_pairs={{0,32},{32,64},{64,96},{96,128},{128,160},{160,192},{192,224},{224... | collective-permute-start | bytes 786440 | tf_op jit(solution)/shard_map/while/body/eval_jaxpr/ppermute | solution.py:19
  1198.7 10.7 collective-permute-start.1
  1217.9 11.3 collective-permute-done.2
  1280.4 12.3 collective-permute-done.2
  1308.9 10.7 collective-permute-start
  1348.5 11.2 collective-permute-start.3
  1393.4 12.7 collective-permute-done.2
  1419.9 130.6 %all-reduce = f32[7,128]{1,0:T(8,128)S(1)} all-reduce(f32[7,128]{1,0:T(8,128)S(1)} %get-tuple-element.298), channel_id=2, replica_groups=mesh['section'=16,'tm'=32] {'section'}, use_global_device_ids=true, to_apply=%region_13.14.clone | all-reduce | flops 896 | bytes 7168
  (888 shorter events, 1008.3 us)
Async XLA Ops:
  6.5 67.7 %all-gather.2.cloned.1.call-start = ((), (), s32[]{:S(2)}) async-start(), calls=%async_computation | async-start | bytes 1949696 | tf_op jit(solution)/shard_map/all_gather | solution.py:170
  92.1 36.4 %collective-permute-start.2 = (f32[128,512]{1,0:T(8,128)S(1)}, f32[128,512]{1,0:T(8,128)S(1)}, u32[]{:S(2)}, u32[]{:S(2)}) collective-permute-start(f32[128,512]{1,0:T(8,128)S(1)} %bitcast.72), channel_id=1, source_target_pairs={{0,16},{1,17},{2,18},{3,19},{4,20},{5,21},{6,22},{7,23},{8,24},{9,... | collective-permute-start | bytes 786440 | tf_op jit(solution)/shard_map/while/body/eval_jaxpr/ppermute | solution.py:25
  158.9 23.7 %collective-permute-start.2 = (f32[128,512]{1,0:T(8,128)S(1)}, f32[128,512]{1,0:T(8,128)S(1)}, u32[]{:S(2)}, u32[]{:S(2)}) collective-permute-start(f32[128,512]{1,0:T(8,128)S(1)} %bitcast.72), channel_id=1, source_target_pairs={{0,16},{1,17},{2,18},{3,19},{4,20},{5,21},{6,22},{7,23},{8,24},{9,... | collective-permute-start | bytes 786440 | tf_op jit(solution)/shard_map/while/body/eval_jaxpr/ppermute | solution.py:25
  208.1 29.3 %collective-permute-start = (f32[128,512]{0,1:T(8,128)S(1)}, f32[128,512]{0,1:T(8,128)}, u32[]{:S(2)}, u32[]{:S(2)}) collective-permute-start(f32[128,512]{0,1:T(8,128)S(1)} %pad_maximum_fusion.8), channel_id=1, source_target_pairs={{0,1},{1,2},{2,3},{3,4},{4,5},{5,6},{6,7},{7,8},{8,9},{9,10},{10,1... | collective-permute-start | bytes 786440 | tf_op jit(solution)/shard_map/while/body/eval_jaxpr/ppermute | solution.py:19
  210.2 34.5 %collective-permute-start.1 = (f32[128,512]{0,1:T(8,128)S(1)}, f32[128,512]{0,1:T(8,128)}, u32[]{:S(2)}, u32[]{:S(2)}) collective-permute-start(f32[128,512]{0,1:T(8,128)S(1)} %pad_maximum_fusion.8), channel_id=1, source_target_pairs={{0,2},{1,3},{2,4},{3,5},{4,6},{5,7},{6,8},{7,9},{8,10},{9,11},{10,... | collective-permute-start | bytes 786440 | tf_op jit(solution)/shard_map/while/body/eval_jaxpr/ppermute | solution.py:19
  231.6 23.7 %collective-permute-start.2 = (f32[128,512]{1,0:T(8,128)S(1)}, f32[128,512]{1,0:T(8,128)S(1)}, u32[]{:S(2)}, u32[]{:S(2)}) collective-permute-start(f32[128,512]{1,0:T(8,128)S(1)} %bitcast.72), channel_id=1, source_target_pairs={{0,16},{1,17},{2,18},{3,19},{4,20},{5,21},{6,22},{7,23},{8,24},{9,... | collective-permute-start | bytes 786440 | tf_op jit(solution)/shard_map/while/body/eval_jaxpr/ppermute | solution.py:25
  292.0 23.1 %collective-permute-start.1 = (f32[128,512]{0,1:T(8,128)S(1)}, f32[128,512]{0,1:T(8,128)}, u32[]{:S(2)}, u32[]{:S(2)}) collective-permute-start(f32[128,512]{0,1:T(8,128)S(1)} %pad_maximum_fusion.8), channel_id=1, source_target_pairs={{0,2},{1,3},{2,4},{3,5},{4,6},{5,7},{6,8},{7,9},{8,10},{9,11},{10,... | collective-permute-start | bytes 786440 | tf_op jit(solution)/shard_map/while/body/eval_jaxpr/ppermute | solution.py:19
  297.2 30.2 %collective-permute-start.2 = (f32[128,512]{1,0:T(8,128)S(1)}, f32[128,512]{1,0:T(8,128)S(1)}, u32[]{:S(2)}, u32[]{:S(2)}) collective-permute-start(f32[128,512]{1,0:T(8,128)S(1)} %bitcast.72), channel_id=1, source_target_pairs={{0,16},{1,17},{2,18},{3,19},{4,20},{5,21},{6,22},{7,23},{8,24},{9,... | collective-permute-start | bytes 786440 | tf_op jit(solution)/shard_map/while/body/eval_jaxpr/ppermute | solution.py:25
  361.4 29.6 %collective-permute-start.2 = (f32[128,512]{1,0:T(8,128)S(1)}, f32[128,512]{1,0:T(8,128)S(1)}, u32[]{:S(2)}, u32[]{:S(2)}) collective-permute-start(f32[128,512]{1,0:T(8,128)S(1)} %bitcast.72), channel_id=1, source_target_pairs={{0,16},{1,17},{2,18},{3,19},{4,20},{5,21},{6,22},{7,23},{8,24},{9,... | collective-permute-start | bytes 786440 | tf_op jit(solution)/shard_map/while/body/eval_jaxpr/ppermute | solution.py:25
  492.3 23.0 %collective-permute-start.2 = (f32[128,512]{1,0:T(8,128)S(1)}, f32[128,512]{1,0:T(8,128)S(1)}, u32[]{:S(2)}, u32[]{:S(2)}) collective-permute-start(f32[128,512]{1,0:T(8,128)S(1)} %bitcast.72), channel_id=1, source_target_pairs={{0,16},{1,17},{2,18},{3,19},{4,20},{5,21},{6,22},{7,23},{8,24},{9,... | collective-permute-start | bytes 786440 | tf_op jit(solution)/shard_map/while/body/eval_jaxpr/ppermute | solution.py:25
  542.9 23.3 %collective-permute-start.1 = (f32[128,512]{0,1:T(8,128)S(1)}, f32[128,512]{0,1:T(8,128)}, u32[]{:S(2)}, u32[]{:S(2)}) collective-permute-start(f32[128,512]{0,1:T(8,128)S(1)} %pad_maximum_fusion.8), channel_id=1, source_target_pairs={{0,2},{1,3},{2,4},{3,5},{4,6},{5,7},{6,8},{7,9},{8,10},{9,11},{10,... | collective-permute-start | bytes 786440 | tf_op jit(solution)/shard_map/while/body/eval_jaxpr/ppermute | solution.py:19
  577.8 22.6 %collective-permute-start.3 = (bf16[128,1024]{1,0:T(8,128)(2,1)S(1)}, bf16[128,1024]{1,0:T(8,128)(2,1)S(1)}, u32[]{:S(2)}, u32[]{:S(2)}) collective-permute-start(bf16[128,1024]{1,0:T(8,128)(2,1)S(1)} %get-tuple-element.576), channel_id=1, source_target_pairs={{0,32},{32,64},{64,96},{96,128},{128,160},{160,192},{192,224},{224... | collective-permute-start | bytes 786440 | tf_op jit(solution)/shard_map/while/body/eval_jaxpr/ppermute | solution.py:19
  605.4 24.1 %collective-permute-start = (f32[128,512]{0,1:T(8,128)S(1)}, f32[128,512]{0,1:T(8,128)}, u32[]{:S(2)}, u32[]{:S(2)}) collective-permute-start(f32[128,512]{0,1:T(8,128)S(1)} %pad_maximum_fusion.8), channel_id=1, source_target_pairs={{0,1},{1,2},{2,3},{3,4},{4,5},{5,6},{6,7},{7,8},{8,9},{9,10},{10,1... | collective-permute-start | bytes 786440 | tf_op jit(solution)/shard_map/while/body/eval_jaxpr/ppermute | solution.py:19
  650.6 30.9 %collective-permute-start = (f32[128,512]{0,1:T(8,128)S(1)}, f32[128,512]{0,1:T(8,128)}, u32[]{:S(2)}, u32[]{:S(2)}) collective-permute-start(f32[128,512]{0,1:T(8,128)S(1)} %pad_maximum_fusion.8), channel_id=1, source_target_pairs={{0,1},{1,2},{2,3},{3,4},{4,5},{5,6},{6,7},{7,8},{8,9},{9,10},{10,1... | collective-permute-start | bytes 786440 | tf_op jit(solution)/shard_map/while/body/eval_jaxpr/ppermute | solution.py:19
  676.0 23.2 %collective-permute-start.2 = (f32[128,512]{1,0:T(8,128)S(1)}, f32[128,512]{1,0:T(8,128)S(1)}, u32[]{:S(2)}, u32[]{:S(2)}) collective-permute-start(f32[128,512]{1,0:T(8,128)S(1)} %bitcast.72), channel_id=1, source_target_pairs={{0,16},{1,17},{2,18},{3,19},{4,20},{5,21},{6,22},{7,23},{8,24},{9,... | collective-permute-start | bytes 786440 | tf_op jit(solution)/shard_map/while/body/eval_jaxpr/ppermute | solution.py:25
  729.0 23.6 %collective-permute-start.1 = (f32[128,512]{0,1:T(8,128)S(1)}, f32[128,512]{0,1:T(8,128)}, u32[]{:S(2)}, u32[]{:S(2)}) collective-permute-start(f32[128,512]{0,1:T(8,128)S(1)} %pad_maximum_fusion.8), channel_id=1, source_target_pairs={{0,2},{1,3},{2,4},{3,5},{4,6},{5,7},{6,8},{7,9},{8,10},{9,11},{10,... | collective-permute-start | bytes 786440 | tf_op jit(solution)/shard_map/while/body/eval_jaxpr/ppermute | solution.py:19
  775.4 24.6 %collective-permute-start = (f32[128,512]{0,1:T(8,128)S(1)}, f32[128,512]{0,1:T(8,128)}, u32[]{:S(2)}, u32[]{:S(2)}) collective-permute-start(f32[128,512]{0,1:T(8,128)S(1)} %pad_maximum_fusion.8), channel_id=1, source_target_pairs={{0,1},{1,2},{2,3},{3,4},{4,5},{5,6},{6,7},{7,8},{8,9},{9,10},{10,1... | collective-permute-start | bytes 786440 | tf_op jit(solution)/shard_map/while/body/eval_jaxpr/ppermute | solution.py:19
  794.0 25.7 %collective-permute-start.2 = (f32[128,512]{1,0:T(8,128)S(1)}, f32[128,512]{1,0:T(8,128)S(1)}, u32[]{:S(2)}, u32[]{:S(2)}) collective-permute-start(f32[128,512]{1,0:T(8,128)S(1)} %bitcast.72), channel_id=1, source_target_pairs={{0,16},{1,17},{2,18},{3,19},{4,20},{5,21},{6,22},{7,23},{8,24},{9,... | collective-permute-start | bytes 786440 | tf_op jit(solution)/shard_map/while/body/eval_jaxpr/ppermute | solution.py:25
  845.6 24.7 %collective-permute-start = (f32[128,512]{0,1:T(8,128)S(1)}, f32[128,512]{0,1:T(8,128)}, u32[]{:S(2)}, u32[]{:S(2)}) collective-permute-start(f32[128,512]{0,1:T(8,128)S(1)} %pad_maximum_fusion.8), channel_id=1, source_target_pairs={{0,1},{1,2},{2,3},{3,4},{4,5},{5,6},{6,7},{7,8},{8,9},{9,10},{10,1... | collective-permute-start | bytes 786440 | tf_op jit(solution)/shard_map/while/body/eval_jaxpr/ppermute | solution.py:19
  851.9 23.2 %collective-permute-start.1 = (f32[128,512]{0,1:T(8,128)S(1)}, f32[128,512]{0,1:T(8,128)}, u32[]{:S(2)}, u32[]{:S(2)}) collective-permute-start(f32[128,512]{0,1:T(8,128)S(1)} %pad_maximum_fusion.8), channel_id=1, source_target_pairs={{0,2},{1,3},{2,4},{3,5},{4,6},{5,7},{6,8},{7,9},{8,10},{9,11},{10,... | collective-permute-start | bytes 786440 | tf_op jit(solution)/shard_map/while/body/eval_jaxpr/ppermute | solution.py:19
  862.2 23.7 %collective-permute-start.2 = (f32[128,512]{1,0:T(8,128)S(1)}, f32[128,512]{1,0:T(8,128)S(1)}, u32[]{:S(2)}, u32[]{:S(2)}) collective-permute-start(f32[128,512]{1,0:T(8,128)S(1)} %bitcast.72), channel_id=1, source_target_pairs={{0,16},{1,17},{2,18},{3,19},{4,20},{5,21},{6,22},{7,23},{8,24},{9,... | collective-permute-start | bytes 786440 | tf_op jit(solution)/shard_map/while/body/eval_jaxpr/ppermute | solution.py:25
  938.5 23.5 %collective-permute-start.3 = (bf16[128,1024]{1,0:T(8,128)(2,1)S(1)}, bf16[128,1024]{1,0:T(8,128)(2,1)S(1)}, u32[]{:S(2)}, u32[]{:S(2)}) collective-permute-start(bf16[128,1024]{1,0:T(8,128)(2,1)S(1)} %get-tuple-element.576), channel_id=1, source_target_pairs={{0,32},{32,64},{64,96},{96,128},{128,160},{160,192},{192,224},{224... | collective-permute-start | bytes 786440 | tf_op jit(solution)/shard_map/while/body/eval_jaxpr/ppermute | solution.py:19
  970.3 22.4 %collective-permute-start.1 = (f32[128,512]{0,1:T(8,128)S(1)}, f32[128,512]{0,1:T(8,128)}, u32[]{:S(2)}, u32[]{:S(2)}) collective-permute-start(f32[128,512]{0,1:T(8,128)S(1)} %pad_maximum_fusion.8), channel_id=1, source_target_pairs={{0,2},{1,3},{2,4},{3,5},{4,6},{5,7},{6,8},{7,9},{8,10},{9,11},{10,... | collective-permute-start | bytes 786440 | tf_op jit(solution)/shard_map/while/body/eval_jaxpr/ppermute | solution.py:19
  1018.7 23.1 %collective-permute-start = (f32[128,512]{0,1:T(8,128)S(1)}, f32[128,512]{0,1:T(8,128)}, u32[]{:S(2)}, u32[]{:S(2)}) collective-permute-start(f32[128,512]{0,1:T(8,128)S(1)} %pad_maximum_fusion.8), channel_id=1, source_target_pairs={{0,1},{1,2},{2,3},{3,4},{4,5},{5,6},{6,7},{7,8},{8,9},{9,10},{10,1... | collective-permute-start | bytes 786440 | tf_op jit(solution)/shard_map/while/body/eval_jaxpr/ppermute | solution.py:19
  1080.8 22.8 %collective-permute-start = (f32[128,512]{0,1:T(8,128)S(1)}, f32[128,512]{0,1:T(8,128)}, u32[]{:S(2)}, u32[]{:S(2)}) collective-permute-start(f32[128,512]{0,1:T(8,128)S(1)} %pad_maximum_fusion.8), channel_id=1, source_target_pairs={{0,1},{1,2},{2,3},{3,4},{4,5},{5,6},{6,7},{7,8},{8,9},{9,10},{10,1... | collective-permute-start | bytes 786440 | tf_op jit(solution)/shard_map/while/body/eval_jaxpr/ppermute | solution.py:19
  1194.2 22.6 %collective-permute-start = (f32[128,512]{0,1:T(8,128)S(1)}, f32[128,512]{0,1:T(8,128)}, u32[]{:S(2)}, u32[]{:S(2)}) collective-permute-start(f32[128,512]{0,1:T(8,128)S(1)} %pad_maximum_fusion.8), channel_id=1, source_target_pairs={{0,1},{1,2},{2,3},{3,4},{4,5},{5,6},{6,7},{7,8},{8,9},{9,10},{10,1... | collective-permute-start | bytes 786440 | tf_op jit(solution)/shard_map/while/body/eval_jaxpr/ppermute | solution.py:19
  1247.3 23.3 %collective-permute-start = (f32[128,512]{0,1:T(8,128)S(1)}, f32[128,512]{0,1:T(8,128)}, u32[]{:S(2)}, u32[]{:S(2)}) collective-permute-start(f32[128,512]{0,1:T(8,128)S(1)} %pad_maximum_fusion.8), channel_id=1, source_target_pairs={{0,1},{1,2},{2,3},{3,4},{4,5},{5,6},{6,7},{7,8},{8,9},{9,10},{10,1... | collective-permute-start | bytes 786440 | tf_op jit(solution)/shard_map/while/body/eval_jaxpr/ppermute | solution.py:19
  1255.3 24.0 %collective-permute-start.1 = (f32[128,512]{0,1:T(8,128)S(1)}, f32[128,512]{0,1:T(8,128)}, u32[]{:S(2)}, u32[]{:S(2)}) collective-permute-start(f32[128,512]{0,1:T(8,128)S(1)} %pad_maximum_fusion.8), channel_id=1, source_target_pairs={{0,2},{1,3},{2,4},{3,5},{4,6},{5,7},{6,8},{7,9},{8,10},{9,11},{10,... | collective-permute-start | bytes 786440 | tf_op jit(solution)/shard_map/while/body/eval_jaxpr/ppermute | solution.py:19
  1264.8 27.9 %collective-permute-start.2 = (f32[128,512]{1,0:T(8,128)S(1)}, f32[128,512]{1,0:T(8,128)S(1)}, u32[]{:S(2)}, u32[]{:S(2)}) collective-permute-start(f32[128,512]{1,0:T(8,128)S(1)} %bitcast.72), channel_id=1, source_target_pairs={{0,16},{1,17},{2,18},{3,19},{4,20},{5,21},{6,22},{7,23},{8,24},{9,... | collective-permute-start | bytes 786440 | tf_op jit(solution)/shard_map/while/body/eval_jaxpr/ppermute | solution.py:25
  1308.9 23.3 %collective-permute-start = (f32[128,512]{0,1:T(8,128)S(1)}, f32[128,512]{0,1:T(8,128)}, u32[]{:S(2)}, u32[]{:S(2)}) collective-permute-start(f32[128,512]{0,1:T(8,128)S(1)} %pad_maximum_fusion.8), channel_id=1, source_target_pairs={{0,1},{1,2},{2,3},{3,4},{4,5},{5,6},{6,7},{7,8},{8,9},{9,10},{10,1... | collective-permute-start | bytes 786440 | tf_op jit(solution)/shard_map/while/body/eval_jaxpr/ppermute | solution.py:19
  1369.8 22.5 %collective-permute-start = (f32[128,512]{0,1:T(8,128)S(1)}, f32[128,512]{0,1:T(8,128)}, u32[]{:S(2)}, u32[]{:S(2)}) collective-permute-start(f32[128,512]{0,1:T(8,128)S(1)} %pad_maximum_fusion.8), channel_id=1, source_target_pairs={{0,1},{1,2},{2,3},{3,4},{4,5},{5,6},{6,7},{7,8},{8,9},{9,10},{10,1... | collective-permute-start | bytes 786440 | tf_op jit(solution)/shard_map/while/body/eval_jaxpr/ppermute | solution.py:19
  1382.9 23.2 %collective-permute-start.2 = (f32[128,512]{1,0:T(8,128)S(1)}, f32[128,512]{1,0:T(8,128)S(1)}, u32[]{:S(2)}, u32[]{:S(2)}) collective-permute-start(f32[128,512]{1,0:T(8,128)S(1)} %bitcast.72), channel_id=1, source_target_pairs={{0,16},{1,17},{2,18},{3,19},{4,20},{5,21},{6,22},{7,23},{8,24},{9,... | collective-permute-start | bytes 786440 | tf_op jit(solution)/shard_map/while/body/eval_jaxpr/ppermute | solution.py:25
  (115 other events, 2705.9 us)
Sparse Core Ops, SparseCore 0:
  10.4 63.8 all-gather.1
where the time goes:
time: 1580 us; the launch traced here: 1560 us
  starting transfers between devices  635 us (40%)
  waiting for transfers between devices  494 us (31%)
  blocking collectives  131 us (8%)
  local copies, waits for them, and re-layouts  107 us (7%)
  other arithmetic  79 us (5%)
  loops' own time  50.8 us (3%)
  matrix products  47.3 us (3%)
    ppermute x66, starting transfers between devices, from_behind(): lax.ppermute(value, axis, [(source, source + steps) for source in range(l...  492 us
    ppermute x22, waiting for transfers between devices, passed_along(): return lax.ppermute(value, axis, pairs)  239 us
    ppermute x66, waiting for transfers between devices, from_behind(): lax.ppermute(value, axis, [(source, source + steps) for source in range(l...  192 us
    ppermute x22, starting transfers between devices, passed_along(): return lax.ppermute(value, axis, pairs)  143 us
    unnamed x1, blocking collectives  131 us
    all_gather x1, waiting for transfers between devices, local(): whole_series = lax.all_gather(series, 'section', axis=2, tiled=True)  63 us
    another operation x1, loops' own time, local(): final_state, totals = lax.fori_loop(0, tick_count, tick_all, initial)  49 us
  transfers between devices with their start and end apart: 89, of which 61 were waited for; matrix products, arithmetic and copies ran while one was open for 5% of the time, Pallas kernels for 0%

commit v1 on v0

v1 whole, which is shorter than its diff:
```python
import functools

import jax
import jax.numpy as jnp
from jax import lax
from jax.experimental import pallas as pl
from jax.experimental.pallas import tpu as pltpu
from jax.sharding import PartitionSpec as P

HEADS = 4
HD = 64
BLK = 64
EPSILON = 1e-05
LAYERS = 16
MICRO = 7
ROWS = 128
D = 1024
NEAR = HEADS * HD
SLOTS = 8
AHEAD = 3
Z = 16
MESH = pl.DeviceIdType.MESH
BF = jnp.bfloat16
F32 = jnp.float32
NEG = -1e30


def compute_section(b):
    y = b // 2
    return 4 * y + 2 * (b % 2) + y % 2


def relay_section(w):
    y = w // 2
    return 4 * y + 2 * (w % 2) + 1 - y % 2


def colour(section):
    x, y = section % 4, section // 4
    return 2 * (y % 2) + (x // 2 + y // 2) % 2


def landed(ref, sem):
    pltpu.make_async_copy(ref, ref, sem).wait()


def dot(a, b):
    return jnp.dot(a, b, preferred_element_type=F32)


def scores_of(q, k):
    return lax.dot_general(q, k, (((1,), (1,)), ((), ())), preferred_element_type=F32)


def attend(q, parts):
    scores = []
    for keys, _, mask in parts:
        s = scores_of(q, keys)
        scores.append(s if mask is None else jnp.where(mask, s, NEG))
    top = functools.reduce(jnp.maximum, scores)
    top = jnp.max(top, axis=-1, keepdims=True)
    raised = [jnp.exp(s - top) for s in scores]
    total = jnp.sum(functools.reduce(jnp.add, raised), axis=-1, keepdims=True)
    out = functools.reduce(
        jnp.add, [dot(p.astype(BF), v) for p, (_, v, _) in zip(raised, parts)]
    )
    return (out / total).astype(BF)


def kernel(
    series, wqkv, wout, gain, readv, dil, order, out,
    stage, ser_rx, h, grs, wq, wo, relay_q, relay_o, near_rx, far_rx, near_own, far_own, qs, heads, totals, out_rx,
    ser_send, ser_recv, gr_send, gr_recv, root_send, relay_recv, rl_send, w_recv, fw_send, fw_recv,
    near_send, near_recv, far_send, far_recv, out_send, out_recv, credit,
):
    sec = lax.axis_index("section")
    tm = lax.axis_index("tm")
    x, y = sec % 4, sec // 4
    z, c = tm // 2, tm % 2
    is_compute = (x + y) % 2 == 0
    micro = 2 * y + x // 2
    shard = Z * c + z
    sibling = (sec, 2 * z + 1 - c)
    neighbours = (
        4 * y + (x + 1) % 4,
        4 * y + (x + 3) % 4,
        4 * ((y + 1) % 4) + x,
        4 * ((y + 3) % 4) + x,
    )

    def copy(src, dst, send, recv, device):
        return pltpu.make_async_remote_copy(
            src_ref=src, dst_ref=dst, send_sem=send, recv_sem=recv, device_id=device, device_id_type=MESH
        )

    def send_or_keep(src, dst, send, recv, device):
        here = (device[0] == sec) & (device[1] == tm)

        @pl.when(here)
        def _():
            pltpu.make_async_copy(src, dst, recv).start()

        @pl.when(jnp.logical_not(here))
        def _():
            copy(src, dst, send, recv, device).start()

    def sent_unless_kept(src, dst, send, recv, device):
        here = (device[0] == sec) & (device[1] == tm)

        @pl.when(jnp.logical_not(here))
        def _():
            copy(src, dst, send, recv, device).wait_send()

    home = 2 * (tm % Z) + tm // Z

    def series_copy(b):
        m = jnp.minimum(b, MICRO - 1)
        return (stage.at[m], ser_rx.at[sec], ser_send.at[b], ser_recv.at[sec], (compute_section(b), home))

    def gain_copy(b):
        return (gain, grs.at[sec, 0], gr_send.at[b, 0], gr_recv.at[sec, 0], (compute_section(b), tm))

    def readv_copy(b):
        return (readv, grs.at[sec, 1], gr_send.at[b, 1], gr_recv.at[sec, 1], (compute_section(b), tm))

    def root_copies(w):
        to = relay_section(w)
        e = 4 * c + colour(to)
        device = (to, tm)
        return (
            (wqkv.at[0, pl.ds(pl.multiple_of(e * 128, 128), 128)], relay_q.at[sec], root_send.at[w, 0], relay_recv.at[sec, 0], device),
            (wout.at[0, pl.ds(pl.multiple_of(e * 64, 64), 64)], relay_o.at[sec], root_send.at[w, 1], relay_recv.at[sec, 1], device),
        )

    def root_start():
        @pl.loop(0, 8)
        def _(w):
            for args in root_copies(w):
                send_or_keep(*args)

    first_step = jnp.maximum(sec - AHEAD, 0)

    for m in range(MICRO):
        slot_of = jnp.full((ROWS, 64), order[m], jnp.int32)
        picked = series[0].astype(F32)
        for k in range(1, MICRO):
            picked = jnp.where(slot_of == k, series[k].astype(F32), picked)
        stage[m] = picked.astype(BF)

    @pl.when(first_step == 0)
    def _():
        root_start()

    @pl.loop(0, 8)
    def _(b):
        send_or_keep(*series_copy(b))
        send_or_keep(*gain_copy(b))
        send_or_keep(*readv_copy(b))

    mine = colour(sec)
    eighth = 4 * c + mine

    def relay_copies(step, j):
        slot = step % SLOTS
        device = (neighbours[j], tm)
        return (
            copy(relay_q.at[step], wq.at[slot, pl.ds(pl.multiple_of(eighth * 128, 128), 128)], rl_send.at[step, j, 0], w_recv.at[slot, mine, 0], device),
            copy(relay_o.at[step], wo.at[slot, pl.ds(pl.multiple_of(eighth * 64, 64), 64)], rl_send.at[step, j, 1], w_recv.at[slot, mine, 1], device),
        )

    @pl.when(jnp.logical_not(is_compute))
    def _():
        @pl.loop(0, LAYERS)
        def _(step):
            @pl.when((step == first_step) & (step > 0))
            def _():
                root_start()

            @pl.when(step >= SLOTS)
            def _():
                for j in range(4):
                    pl.semaphore_wait(credit.at[j], 1)

            landed(relay_q.at[step], relay_recv.at[step, 0])
            for j in range(4):
                relay_copies(step, j)[0].start()
            landed(relay_o.at[step], relay_recv.at[step, 1])
            for j in range(4):
                relay_copies(step, j)[1].start()

        @pl.loop(0, LAYERS)
        def _(step):
            for j in range(4):
                for one in relay_copies(step, j):
                    one.wait_send()

    def half_copies(step):
        slot = step % SLOTS
        half_q = wq.at[slot, pl.ds(pl.multiple_of(c * 512, 512), 512)]
        half_o = wo.at[slot, pl.ds(pl.multiple_of(c * 256, 256), 256)]
        return (
            copy(half_q, half_q, fw_send.at[slot, 0], fw_recv.at[slot, 0], sibling),
            copy(half_o, half_o, fw_send.at[slot, 1], fw_recv.at[slot, 1], sibling),
        )

    def landed_half(step, part):
        slot = step % SLOTS
        landed((wq.at[slot, pl.ds(0, 512)], wo.at[slot, pl.ds(0, 256)])[part], fw_recv.at[slot, part])

    def share_half(step):
        slot = step % SLOTS
        for q in range(4):
            e = 4 * c + q
            landed(wq.at[slot, pl.ds(pl.multiple_of(e * 128, 128), 128)], w_recv.at[slot, q, 0])
        half_copies(step)[0].start()
        for q in range(4):
            e = 4 * c + q
            landed(wo.at[slot, pl.ds(pl.multiple_of(e * 64, 64), 64)], w_recv.at[slot, q, 1])
        half_copies(step)[1].start()

    def near_copy(step, distance):
        other = (shard + distance) % (2 * Z)
        device = (sec, 2 * (other % Z) + other // Z)
        return copy(near_own, near_rx.at[step, distance - 1], near_send.at[distance - 1], near_recv.at[step, distance - 1], device)

    def far_copy(step):
        return copy(far_own, far_rx.at[step], far_send.at[0], far_recv.at[step], sibling)

    def layer(step):
        slot = step % SLOTS

        @pl.when((step == first_step) & (step > 0))
        def _():
            root_start()

        landed_half(step, 0)
        landed(grs.at[step, 0], gr_recv.at[step, 0])
        hidden = h[...].astype(F32)
        scale = lax.rsqrt(jnp.mean(hidden * hidden, axis=-1, keepdims=True) + EPSILON)
        normed = (hidden * scale * grs[step, 0]).astype(BF)
        near_own[:, :NEAR] = dot(normed, wq[slot, :, 512:768]).astype(BF)
        near_own[:, NEAR:] = dot(normed, wq[slot, :, 1024:1280]).astype(BF)
        near_copy(step, 1).start()
        near_copy(step, 2).start()
        far_own[:, :NEAR] = dot(normed, wq[slot, :, 768:1024]).astype(BF)
        far_own[:, NEAR:] = dot(normed, wq[slot, :, 1280:1536]).astype(BF)
        far_copy(step).start()
        qs[...] = (dot(normed, wq[slot, :, :512]) * (HD**-0.5)).astype(BF)

        row = lax.broadcasted_iota(jnp.int32, (ROWS, ROWS), 0)
        col = lax.broadcasted_iota(jnp.int32, (ROWS, ROWS), 1)
        same = (row < BLK) == (col < BLK)
        far_copy(step).wait_recv()
        block = jnp.where(row < BLK, dil[2 * shard], dil[2 * shard + 1])
        wanted = jnp.where(col < BLK, 0, 1) == block
        for head in range(HEADS):
            k = slice(head * HD, (head + 1) * HD)
            v = slice(NEAR + head * HD, NEAR + (head + 1) * HD)
            q = qs[:, NEAR + head * HD : NEAR + (head + 1) * HD]
            heads[:, NEAR + head * HD : NEAR + (head + 1) * HD] = attend(
                q,
                (
                    (far_own[:, k], far_own[:, v], same),
                    (far_rx[step, :, k], far_rx[step, :, v], wanted),
                ),
            )

        @pl.when(step + 1 < LAYERS)
        def _():
            share_half(step + 1)

        near_copy(step, 1).wait_recv()
        near_copy(step, 2).wait_recv()
        oldest = (col > row) & (shard >= 2)
        middle = (col >= 0) & (shard >= 1)
        for head in range(HEADS):
            k = slice(head * HD, (head + 1) * HD)
            v = slice(NEAR + head * HD, NEAR + (head + 1) * HD)
            heads[:, k] = attend(
                qs[:, k],
                (
                    (near_own[:, k], near_own[:, v], col <= row),
                    (near_rx[step, 0, :, k], near_rx[step, 0, :, v], middle),
                    (near_rx[step, 1, :, k], near_rx[step, 1, :, v], oldest),
                ),
            )
        landed_half(step, 1)
        landed(grs.at[step, 1], gr_recv.at[step, 1])
        updated = (h[...].astype(F32) + dot(heads[...], wo[slot])).astype(BF)
        h[...] = updated
        u = updated.astype(F32)
        scale = lax.rsqrt(jnp.mean(u * u, axis=-1, keepdims=True) + EPSILON)
        term = jnp.sum(u * scale * grs[step, 1], axis=-1, keepdims=True)
        totals[...] += jnp.broadcast_to(term, (ROWS, 128))

        near_copy(step, 1).wait_send()
        near_copy(step, 2).wait_send()
        far_copy(step).wait_send()
        for one in half_copies(step):
            one.wait_send()

        @pl.when(step + SLOTS < LAYERS)
        def _():
            for j in range(4):
                pl.semaphore_signal(credit.at[j ^ 1], inc=1, device_id=(neighbours[j], tm), device_id_type=MESH)

    def result_copy(s):
        return (totals.at[pl.ds(pl.multiple_of(8 * s, 8), 8)], out_rx.at[micro], out_send.at[s], out_recv.at[micro], (s, shard))

    @pl.when(is_compute)
    def _():
        totals[...] = jnp.zeros_like(totals)
        for s in range(LAYERS):
            landed(ser_rx.at[s], ser_recv.at[s])
            h[:, s * 64 : (s + 1) * 64] = ser_rx[s]
        share_half(0)

        @pl.loop(0, LAYERS)
        def _(step):
            layer(step)

        @pl.when(micro < MICRO)
        def _():
            @pl.loop(0, LAYERS)
            def _(s):
                send_or_keep(*result_copy(s))

    lane = lax.broadcasted_iota(jnp.int32, (8, 128), 1)
    line = lax.broadcasted_iota(jnp.int32, (8, 128), 0)
    for m in range(MICRO):
        landed(out_rx.at[m], out_recv.at[m])
        turned = jnp.sum(jnp.where(lane == line, out_rx[m], 0.0), axis=0, keepdims=True)
        out[m] = turned[:, :8]

    @pl.when(is_compute & (micro < MICRO))
    def _():
        @pl.loop(0, LAYERS)
        def _(s):
            sent_unless_kept(*result_copy(s))

    @pl.loop(0, 8)
    def _(b):
        sent_unless_kept(*series_copy(b))
        sent_unless_kept(*gain_copy(b))
        sent_unless_kept(*readv_copy(b))
        for args in root_copies(b):
            sent_unless_kept(*args)


def local(series, query_key_value_weight, output_weight, gain, readout_weight, dilation_block, order):
    dma = pltpu.SemaphoreType.DMA
    vmem = pl.BlockSpec(memory_space=pltpu.VMEM)
    hbm = pl.BlockSpec(memory_space=pl.ANY)
    smem = pl.BlockSpec(memory_space=pltpu.SMEM)
    return pl.pallas_call(
        kernel,
        out_shape=jax.ShapeDtypeStruct((MICRO, 1, 8), F32),
        in_specs=[vmem, hbm, hbm, vmem, vmem, smem, smem],
        out_specs=vmem,
        scratch_shapes=[
            pltpu.VMEM((MICRO, ROWS, 64), BF),
            pltpu.VMEM((LAYERS, ROWS, 64), BF),
            pltpu.VMEM((ROWS, D), BF),
            pltpu.VMEM((LAYERS, 2, 1, D), F32),
            pltpu.VMEM((SLOTS, D, 1536), BF),
            pltpu.VMEM((SLOTS, 512, D), BF),
            pltpu.VMEM((LAYERS, 128, 1536), BF),
            pltpu.VMEM((LAYERS, 64, D), BF),
            pltpu.VMEM((LAYERS, 2, ROWS, 2 * NEAR), BF),
            pltpu.VMEM((LAYERS, ROWS, 2 * NEAR), BF),
            pltpu.VMEM((ROWS, 2 * NEAR), BF),
            pltpu.VMEM((ROWS, 2 * NEAR), BF),
            pltpu.VMEM((ROWS, 512), BF),
            pltpu.VMEM((ROWS, 512), BF),
            pltpu.VMEM((ROWS, 128), F32),
            pltpu.VMEM((MICRO, 8, 128), F32),
            dma((8,)), dma((LAYERS,)),
            dma((8, 2)), dma((LAYERS, 2)),
            dma((8, 2)), dma((LAYERS, 2)),
            dma((LAYERS, 4, 2)), dma((SLOTS, 4, 2)),
            dma((SLOTS, 2)), dma((SLOTS, 2)),
            dma((2,)), dma((LAYERS, 2)),
            dma((1,)), dma((LAYERS,)),
            dma((LAYERS,)), dma((MICRO,)),
            pltpu.SemaphoreType.REGULAR((4,)),
        ],
        compiler_params=pltpu.CompilerParams(has_side_effects=True, vmem_limit_bytes=58 * 2**20),
    )(series, query_key_value_weight, output_weight, gain, readout_weight, dilation_block, order)


def solution(mesh):
    placed = (
        P(None, "tm", "section"),
        P("section", None, None),
        P("section", None, None),
        P("section", None),
        P("section", None),
        P(),
        P(),
    )
    return jax.shard_map(
        local, mesh=mesh, in_specs=placed, out_specs=P(None, "tm", "section"), check_vma=False
    )
```

time: 1580 us -> 462 us (0.29)
  the two profiles are of different devices: /device:TPU:1 before, /device:TPU:65 now
where the time goes in v1:
time: 462 us
  Pallas kernels  459 us (99%)
    pallas_call x1, Pallas kernels, local(): pl.pallas_call(kernel, out_shape=jax.ShapeDtypeStruct((MICRO, 1, 8), F32)...  459 us

profile of v1, /device:TPU:65, one launch (start us, length us, event | category | flops | bytes accessed | tf_op | source)
XLA Modules:
  0.0 462.3 jit_solution(17674034152002371479)
XLA Ops:
  0.0 1.7 copy.8.series
  1.7 459.3 %shard_map.73 = f32[7,1,8]{2,1,0:T(1,128)} custom-call(bf16[7,128,64]{2,1,0:T(8,128)(2,1)} %copy.8.series, bf16[1,1024,1536]{2,1,0:T(8,128)(2,1)} %wqkv.1, bf16[1,512,1024]{2,1,0:T(8,128)(2,1)} %wout.1, f32[1,1024]{1,0:T(1,128)} %gain.1, f32[1,1024]{1,0:T(1,128)} %readv.1, s32[64]{0:T(128)} %dil.1, s32[7]{0:T(128)} %order.1), custom_call_target="tpu_custom_call" | custom-call | tf_op jit(solution)/shard_map/pallas_call | solution.py:355
  461.0 1.3 copy.10

commit v2 on v1

--- a/solution.py
+++ b/solution.py
@@ -17,7 +17,7 @@
 D = 1024
 NEAR = HEADS * HD
 SLOTS = 8
-AHEAD = 3
+AHEAD = 4
 Z = 16
 MESH = pl.DeviceIdType.MESH
 BF = jnp.bfloat16
@@ -70,7 +70,7 @@
 def kernel(
     series, wqkv, wout, gain, readv, dil, order, out,
     stage, ser_rx, h, grs, wq, wo, relay_q, relay_o, near_rx, far_rx, near_own, far_own, qs, heads, totals, out_rx,
-    ser_send, ser_recv, gr_send, gr_recv, root_send, relay_recv, rl_send, w_recv, fw_send, fw_recv,
+    ser_send, ser_recv, gr_send, gr_recv, root_send, relay_recv, swap_send, rl_send, w_recv, fw_send, fw_recv,
     near_send, near_recv, far_send, far_recv, out_send, out_recv, credit,
 ):
     sec = lax.axis_index("section")
@@ -123,13 +123,36 @@
     def readv_copy(b):
         return (readv, grs.at[sec, 1], gr_send.at[b, 1], gr_recv.at[sec, 1], (compute_section(b), tm))
 
+    part = z % 4
+
+    def part_q(step, k):
+        return relay_q.at[step, pl.ds(pl.multiple_of(k * 32, 32), 32)]
+
+    def part_o(step, k):
+        return relay_o.at[step, pl.ds(pl.multiple_of(k * 16, 16), 16)]
+
+    def part_copies(step, i):
+        to = (z + (1, Z - 1, Z + 2 - 4 * c)[i]) % Z
+        device = (sec, 2 * to + c)
+        return (
+            copy(part_q(step, part), part_q(step, part), swap_send.at[step, i, 0], relay_recv.at[step, part, 0], device),
+            copy(part_o(step, part), part_o(step, part), swap_send.at[step, i, 1], relay_recv.at[step, part, 1], device),
+        )
+
+    def swap_parts(step):
+        landed(part_q(step, part), relay_recv.at[step, part, 0])
+        landed(part_o(step, part), relay_recv.at[step, part, 1])
+        for i in range(3):
+            for one in part_copies(step, i):
+                one.start()
+
     def root_copies(w):
         to = relay_section(w)
         e = 4 * c + colour(to)
         device = (to, tm)
         return (
-            (wqkv.at[0, pl.ds(pl.multiple_of(e * 128, 128), 128)], relay_q.at[sec], root_send.at[w, 0], relay_recv.at[sec, 0], device),
-            (wout.at[0, pl.ds(pl.multiple_of(e * 64, 64), 64)], relay_o.at[sec], root_send.at[w, 1], relay_recv.at[sec, 1], device),
+            (wqkv.at[0, pl.ds(pl.multiple_of(e * 128 + part * 32, 32), 32)], part_q(sec, part), root_send.at[w, 0], relay_recv.at[sec, part, 0], device),
+            (wout.at[0, pl.ds(pl.multiple_of(e * 64 + part * 16, 16), 16)], part_o(sec, part), root_send.at[w, 1], relay_recv.at[sec, part, 1], device),
         )
 
     def root_start():
@@ -160,16 +183,18 @@
     mine = colour(sec)
     eighth = 4 * c + mine
 
-    def relay_copies(step, j):
-        slot = step % SLOTS
-        device = (neighbours[j], tm)
-        return (
-            copy(relay_q.at[step], wq.at[slot, pl.ds(pl.multiple_of(eighth * 128, 128), 128)], rl_send.at[step, j, 0], w_recv.at[slot, mine, 0], device),
-            copy(relay_o.at[step], wo.at[slot, pl.ds(pl.multiple_of(eighth * 64, 64), 64)], rl_send.at[step, j, 1], w_recv.at[slot, mine, 1], device),
-        )
+    def relay_copy_q(step, j):
+        slot = step % SLOTS
+        return copy(relay_q.at[step], wq.at[slot, pl.ds(pl.multiple_of(eighth * 128, 128), 128)], rl_send.at[step, j, 0], w_recv.at[slot, mine, 0], (neighbours[j], tm))
+
+    def relay_copy_o(step, j):
+        slot = step % SLOTS
+        return copy(relay_o.at[step], wo.at[slot, pl.ds(pl.multiple_of(eighth * 64, 64), 64)], rl_send.at[step, j, 1], w_recv.at[slot, mine, 1], (neighbours[j], tm))
 
     @pl.when(jnp.logical_not(is_compute))
     def _():
+        swap_parts(0)
+
         @pl.loop(0, LAYERS)
         def _(step):
             @pl.when((step == first_step) & (step > 0))
@@ -181,42 +206,52 @@
                 for j in range(4):
                     pl.semaphore_wait(credit.at[j], 1)
 
-            landed(relay_q.at[step], relay_recv.at[step, 0])
+            for d in range(1, 4):
+                k = (part + d) % 4
+                landed(part_q(step, k), relay_recv.at[step, k, 0])
+                landed(part_o(step, k), relay_recv.at[step, k, 1])
             for j in range(4):
-                relay_copies(step, j)[0].start()
-            landed(relay_o.at[step], relay_recv.at[step, 1])
+                relay_copy_q(step, j).start()
             for j in range(4):
-                relay_copies(step, j)[1].start()
+                relay_copy_o(step, j).start()
+
+            @pl.when(step + 1 < LAYERS)
+            def _():
+                swap_parts(step + 1)
 
         @pl.loop(0, LAYERS)
         def _(step):
             for j in range(4):
-                for one in relay_copies(step, j):
+                relay_copy_q(step, j).wait_send()
+                relay_copy_o(step, j).wait_send()
+            for i in range(3):
+                for one in part_copies(step, i):
                     one.wait_send()
 
-    def half_copies(step):
-        slot = step % SLOTS
-        half_q = wq.at[slot, pl.ds(pl.multiple_of(c * 512, 512), 512)]
-        half_o = wo.at[slot, pl.ds(pl.multiple_of(c * 256, 256), 256)]
-        return (
-            copy(half_q, half_q, fw_send.at[slot, 0], fw_recv.at[slot, 0], sibling),
-            copy(half_o, half_o, fw_send.at[slot, 1], fw_recv.at[slot, 1], sibling),
-        )
-
-    def landed_half(step, part):
-        slot = step % SLOTS
-        landed((wq.at[slot, pl.ds(0, 512)], wo.at[slot, pl.ds(0, 256)])[part], fw_recv.at[slot, part])
+    def half_copy_q(step):
+        slot = step % SLOTS
+        half = wq.at[slot, pl.ds(pl.multiple_of(c * 512, 512), 512)]
+        return copy(half, half, fw_send.at[slot, 0], fw_recv.at[slot, 0], sibling)
+
+    def half_copy_o(step):
+        slot = step % SLOTS
+        half = wo.at[slot, pl.ds(pl.multiple_of(c * 256, 256), 256)]
+        return copy(half, half, fw_send.at[slot, 1], fw_recv.at[slot, 1], sibling)
+
+    def landed_half(step, which):
+        slot = step % SLOTS
+        landed((wq.at[slot, pl.ds(0, 512)], wo.at[slot, pl.ds(0, 256)])[which], fw_recv.at[slot, which])
 
     def share_half(step):
         slot = step % SLOTS
         for q in range(4):
             e = 4 * c + q
             landed(wq.at[slot, pl.ds(pl.multiple_of(e * 128, 128), 128)], w_recv.at[slot, q, 0])
-        half_copies(step)[0].start()
+        half_copy_q(step).start()
         for q in range(4):
             e = 4 * c + q
             landed(wo.at[slot, pl.ds(pl.multiple_of(e * 64, 64), 64)], w_recv.at[slot, q, 1])
-        half_copies(step)[1].start()
+        half_copy_o(step).start()
 
     def near_copy(step, distance):
         other = (shard + distance) % (2 * Z)
@@ -296,8 +331,8 @@
         near_copy(step, 1).wait_send()
         near_copy(step, 2).wait_send()
         far_copy(step).wait_send()
-        for one in half_copies(step):
-            one.wait_send()
+        half_copy_q(step).wait_send()
+        half_copy_o(step).wait_send()
 
         @pl.when(step + SLOTS < LAYERS)
         def _():
@@ -376,7 +411,7 @@
             pltpu.VMEM((MICRO, 8, 128), F32),
             dma((8,)), dma((LAYERS,)),
             dma((8, 2)), dma((LAYERS, 2)),
-            dma((8, 2)), dma((LAYERS, 2)),
+            dma((8, 2)), dma((LAYERS, 4, 2)), dma((LAYERS, 3, 2)),
             dma((LAYERS, 4, 2)), dma((SLOTS, 4, 2)),
             dma((SLOTS, 2)), dma((SLOTS, 2)),
             dma((2,)), dma((LAYERS, 2)),

time: 462 us -> 299 us (0.65)
  the two profiles are of different devices: /device:TPU:65 before, /device:TPU:129 now
where the time goes in v2:
time: 299 us; the launch traced here: 298 us
  Pallas kernels  295 us (99%)
    pallas_call x1, Pallas kernels, local(): pl.pallas_call(kernel, out_shape=jax.ShapeDtypeStruct((MICRO, 1, 8), F32)...  295 us

profile of v2, /device:TPU:129, one launch (start us, length us, event | category | flops | bytes accessed | tf_op | source)
XLA Modules:
  0.0 298.4 jit_solution(16538041577546760502)
XLA Ops:
  0.0 1.7 copy.8.series
  1.7 295.4 %shard_map.73 = f32[7,1,8]{2,1,0:T(1,128)} custom-call(bf16[7,128,64]{2,1,0:T(8,128)(2,1)} %copy.8.series, bf16[1,1024,1536]{2,1,0:T(8,128)(2,1)} %wqkv.1, bf16[1,512,1024]{2,1,0:T(8,128)(2,1)} %wout.1, f32[1,1024]{1,0:T(1,128)} %gain.1, f32[1,1024]{1,0:T(1,128)} %readv.1, s32[64]{0:T(128)} %dil.1, s32[7]{0:T(128)} %order.1), custom_call_target="tpu_custom_call" | custom-call | tf_op jit(solution)/shard_map/pallas_call | solution.py:390
  297.1 1.3 copy.10

commit v3 on v2

--- a/solution.py
+++ b/solution.py
@@ -19,6 +19,8 @@
 SLOTS = 8
 AHEAD = 4
 Z = 16
+GREET_COMPUTE = 15 + 16 + 8 + 3
+GREET_RELAY = 15 + 8 + 4
 MESH = pl.DeviceIdType.MESH
 BF = jnp.bfloat16
 F32 = jnp.float32
@@ -52,18 +54,28 @@
     return lax.dot_general(q, k, (((1,), (1,)), ((), ())), preferred_element_type=F32)
 
 
-def attend(q, parts):
+def attend(q, parts, before=None):
     scores = []
     for keys, _, mask in parts:
         s = scores_of(q, keys)
         scores.append(s if mask is None else jnp.where(mask, s, NEG))
-    top = functools.reduce(jnp.maximum, scores)
-    top = jnp.max(top, axis=-1, keepdims=True)
+    top = jnp.max(functools.reduce(jnp.maximum, scores), axis=-1, keepdims=True)
+    if before is not None:
+        top = jnp.maximum(top, before[0])
     raised = [jnp.exp(s - top) for s in scores]
     total = jnp.sum(functools.reduce(jnp.add, raised), axis=-1, keepdims=True)
     out = functools.reduce(
         jnp.add, [dot(p.astype(BF), v) for p, (_, v, _) in zip(raised, parts)]
     )
+    if before is not None:
+        fade = jnp.exp(before[0] - top)
+        total = total + before[1] * fade
+        out = out + before[2] * fade
+    return top, total, out
+
+
+def weighted(state):
+    _, total, out = state
     return (out / total).astype(BF)
 
 
@@ -111,11 +123,51 @@
         def _():
             copy(src, dst, send, recv, device).wait_send()
 
+    def near_device(distance):
+        other = (shard + distance + 2 * Z) % (2 * Z)
+        return (sec, 2 * (other % Z) + other // Z)
+
+    def greet():
+        barrier = pltpu.get_barrier_semaphore()
+
+        def meet(device):
+            here = (device[0] == sec) & (device[1] == tm)
+
+            @pl.when(jnp.logical_not(here))
+            def _():
+                pl.semaphore_signal(barrier, inc=1, device_id=device, device_id_type=MESH)
+
+        @pl.loop(0, LAYERS)
+        def _(s):
+            meet((s, tm))
+
+        @pl.loop(0, 8)
+        def _(b):
+            meet((compute_section(b), home))
+
+        @pl.when(is_compute)
+        def _():
+            @pl.loop(0, LAYERS)
+            def _(s):
+                meet((s, shard))
+
+            meet(sibling)
+            for distance in (-1, 1):
+                meet(near_device(distance))
+
+        @pl.when(jnp.logical_not(is_compute))
+        def _():
+            for far in (1, 2):
+                meet((sec, 2 * ((z + far) % Z) + c))
+                meet((sec, 2 * ((z + Z - far) % Z) + c))
+
+        pl.semaphore_wait(barrier, jnp.where(is_compute, jnp.where(shard == tm, GREET_COMPUTE - 2, GREET_COMPUTE), GREET_RELAY))
+
     home = 2 * (tm % Z) + tm // Z
 
     def series_copy(b):
         m = jnp.minimum(b, MICRO - 1)
-        return (stage.at[m], ser_rx.at[sec], ser_send.at[b], ser_recv.at[sec], (compute_section(b), home))
+        return (stage.at[m], ser_rx.at[pl.ds(pl.multiple_of(sec * 64, 64), 64)], ser_send.at[b], ser_recv.at[sec], (compute_section(b), home))
 
     def gain_copy(b):
         return (gain, grs.at[sec, 0], gr_send.at[b, 0], gr_recv.at[sec, 0], (compute_section(b), tm))
@@ -163,16 +215,18 @@
 
     first_step = jnp.maximum(sec - AHEAD, 0)
 
+    greet()
+
+    @pl.when(first_step == 0)
+    def _():
+        root_start()
+
     for m in range(MICRO):
-        slot_of = jnp.full((ROWS, 64), order[m], jnp.int32)
+        slot_of = jnp.full((64, ROWS), order[m], jnp.int32)
         picked = series[0].astype(F32)
         for k in range(1, MICRO):
             picked = jnp.where(slot_of == k, series[k].astype(F32), picked)
         stage[m] = picked.astype(BF)
-
-    @pl.when(first_step == 0)
-    def _():
-        root_start()
 
     @pl.loop(0, 8)
     def _(b):
@@ -253,10 +307,11 @@
             landed(wo.at[slot, pl.ds(pl.multiple_of(e * 64, 64), 64)], w_recv.at[slot, q, 1])
         half_copy_o(step).start()
 
-    def near_copy(step, distance):
-        other = (shard + distance) % (2 * Z)
-        device = (sec, 2 * (other % Z) + other // Z)
-        return copy(near_own, near_rx.at[step, distance - 1], near_send.at[distance - 1], near_recv.at[step, distance - 1], device)
+    def near_copy(step, kv):
+        return copy(near_own.at[kv], near_rx.at[step, 0, kv], near_send.at[0, kv], near_recv.at[step, 0, kv], near_device(1))
+
+    def near_pass(step, kv):
+        return copy(near_rx.at[step, 0, kv], near_rx.at[step, 1, kv], near_send.at[1, kv], near_recv.at[step, 1, kv], near_device(1))
 
     def far_copy(step):
         return copy(far_own, far_rx.at[step], far_send.at[0], far_recv.at[step], sibling)
@@ -273,10 +328,10 @@
         hidden = h[...].astype(F32)
         scale = lax.rsqrt(jnp.mean(hidden * hidden, axis=-1, keepdims=True) + EPSILON)
         normed = (hidden * scale * grs[step, 0]).astype(BF)
-        near_own[:, :NEAR] = dot(normed, wq[slot, :, 512:768]).astype(BF)
-        near_own[:, NEAR:] = dot(normed, wq[slot, :, 1024:1280]).astype(BF)
+        near_own[0] = dot(normed, wq[slot, :, 512:768]).astype(BF)
+        near_copy(step, 0).start()
+        near_own[1] = dot(normed, wq[slot, :, 1024:1280]).astype(BF)
         near_copy(step, 1).start()
-        near_copy(step, 2).start()
         far_own[:, :NEAR] = dot(normed, wq[slot, :, 768:1024]).astype(BF)
         far_own[:, NEAR:] = dot(normed, wq[slot, :, 1280:1536]).astype(BF)
         far_copy(step).start()
@@ -292,33 +347,43 @@
             k = slice(head * HD, (head + 1) * HD)
             v = slice(NEAR + head * HD, NEAR + (head + 1) * HD)
             q = qs[:, NEAR + head * HD : NEAR + (head + 1) * HD]
-            heads[:, NEAR + head * HD : NEAR + (head + 1) * HD] = attend(
-                q,
-                (
-                    (far_own[:, k], far_own[:, v], same),
-                    (far_rx[step, :, k], far_rx[step, :, v], wanted),
-                ),
+            heads[:, NEAR + head * HD : NEAR + (head + 1) * HD] = weighted(
+                attend(
+                    q,
+                    (
+                        (far_own[:, k], far_own[:, v], same),
+                        (far_rx[step, :, k], far_rx[step, :, v], wanted),
+                    ),
+                )
             )
+        for kv in range(2):
+            near_copy(step, kv).wait_recv()
+            near_pass(step, kv).start()
 
         @pl.when(step + 1 < LAYERS)
         def _():
             share_half(step + 1)
 
-        near_copy(step, 1).wait_recv()
-        near_copy(step, 2).wait_recv()
         oldest = (col > row) & (shard >= 2)
         middle = (col >= 0) & (shard >= 1)
+        begun = []
         for head in range(HEADS):
             k = slice(head * HD, (head + 1) * HD)
-            v = slice(NEAR + head * HD, NEAR + (head + 1) * HD)
-            heads[:, k] = attend(
-                qs[:, k],
-                (
-                    (near_own[:, k], near_own[:, v], col <= row),
-                    (near_rx[step, 0, :, k], near_rx[step, 0, :, v], middle),
-                    (near_rx[step, 1, :, k], near_rx[step, 1, :, v], oldest),
-                ),
+            begun.append(
+                attend(
+                    qs[:, k],
+                    (
+                        (near_own[0, :, k], near_own[1, :, k], col <= row),
+                        (near_rx[step, 0, 0, :, k], near_rx[step, 0, 1, :, k], middle),
+                    ),
+                )
             )
+        for kv in range(2):
+            near_pass(step, kv).wait_recv()
+        for head in range(HEADS):
+            k = slice(head * HD, (head + 1) * HD)
+            last = (near_rx[step, 1, 0, :, k], near_rx[step, 1, 1, :, k], oldest)
+            heads[:, k] = weighted(attend(qs[:, k], (last,), begun[head]))
         landed_half(step, 1)
         landed(grs.at[step, 1], gr_recv.at[step, 1])
         updated = (h[...].astype(F32) + dot(heads[...], wo[slot])).astype(BF)
@@ -328,8 +393,9 @@
         term = jnp.sum(u * scale * grs[step, 1], axis=-1, keepdims=True)
         totals[...] += jnp.broadcast_to(term, (ROWS, 128))
 
-        near_copy(step, 1).wait_send()
-        near_copy(step, 2).wait_send()
+        for kv in range(2):
+            near_copy(step, kv).wait_send()
+            near_pass(step, kv).wait_send()
         far_copy(step).wait_send()
         half_copy_q(step).wait_send()
         half_copy_o(step).wait_send()
@@ -346,8 +412,10 @@
     def _():
         totals[...] = jnp.zeros_like(totals)
         for s in range(LAYERS):
-            landed(ser_rx.at[s], ser_recv.at[s])
-            h[:, s * 64 : (s + 1) * 64] = ser_rx[s]
+            landed(ser_rx.at[pl.ds(s * 64, 64)], ser_recv.at[s])
+        for i in range(D // 128):
+            block = slice(i * 128, (i + 1) * 128)
+            h[:, block] = ser_rx[block, :].astype(F32).T.astype(BF)
         share_half(0)
 
         @pl.loop(0, LAYERS)
@@ -393,17 +461,17 @@
         in_specs=[vmem, hbm, hbm, vmem, vmem, smem, smem],
         out_specs=vmem,
         scratch_shapes=[
-            pltpu.VMEM((MICRO, ROWS, 64), BF),
-            pltpu.VMEM((LAYERS, ROWS, 64), BF),
+            pltpu.VMEM((MICRO, 64, ROWS), BF),
+            pltpu.VMEM((D, ROWS), BF),
             pltpu.VMEM((ROWS, D), BF),
             pltpu.VMEM((LAYERS, 2, 1, D), F32),
             pltpu.VMEM((SLOTS, D, 1536), BF),
             pltpu.VMEM((SLOTS, 512, D), BF),
             pltpu.VMEM((LAYERS, 128, 1536), BF),
             pltpu.VMEM((LAYERS, 64, D), BF),
-            pltpu.VMEM((LAYERS, 2, ROWS, 2 * NEAR), BF),
+            pltpu.VMEM((LAYERS, 2, 2, ROWS, NEAR), BF),
             pltpu.VMEM((LAYERS, ROWS, 2 * NEAR), BF),
-            pltpu.VMEM((ROWS, 2 * NEAR), BF),
+            pltpu.VMEM((2, ROWS, NEAR), BF),
             pltpu.VMEM((ROWS, 2 * NEAR), BF),
             pltpu.VMEM((ROWS, 512), BF),
             pltpu.VMEM((ROWS, 512), BF),
@@ -414,13 +482,13 @@
             dma((8, 2)), dma((LAYERS, 4, 2)), dma((LAYERS, 3, 2)),
             dma((LAYERS, 4, 2)), dma((SLOTS, 4, 2)),
             dma((SLOTS, 2)), dma((SLOTS, 2)),
-            dma((2,)), dma((LAYERS, 2)),
+            dma((2, 2)), dma((LAYERS, 2, 2)),
             dma((1,)), dma((LAYERS,)),
             dma((LAYERS,)), dma((MICRO,)),
             pltpu.SemaphoreType.REGULAR((4,)),
         ],
-        compiler_params=pltpu.CompilerParams(has_side_effects=True, vmem_limit_bytes=58 * 2**20),
-    )(series, query_key_value_weight, output_weight, gain, readout_weight, dilation_block, order)
+        compiler_params=pltpu.CompilerParams(collective_id=0, has_side_effects=True, vmem_limit_bytes=58 * 2**20),
+    )(jnp.swapaxes(series, 1, 2), query_key_value_weight, output_weight, gain, readout_weight, dilation_block, order)
 
 
 def solution(mesh):

time: 299 us -> 272 us (0.910)
  the two profiles are of different devices: /device:TPU:129 before, /device:TPU:1 now
where the time goes in v3:
time: 272 us; the launch traced here: 268 us
  Pallas kernels  267 us (98%)
    pallas_call x1, Pallas kernels, local(): pl.pallas_call(kernel, out_shape=jax.ShapeDtypeStruct((MICRO, 1, 8), F32)...  267 us

profile of v3, /device:TPU:1, one launch (start us, length us, event | category | flops | bytes accessed | tf_op | source)
XLA Modules:
  0.0 268.3 jit_solution(13992446143351159315)
XLA Ops:
  0.0 267.0 %shard_map.73 = f32[7,1,8]{2,1,0:T(1,128)} custom-call(bf16[7,64,128]{2,1,0:T(8,128)(2,1)} %bitcast.1, bf16[1,1024,1536]{2,1,0:T(8,128)(2,1)} %wqkv.1, bf16[1,512,1024]{2,1,0:T(8,128)(2,1)} %wout.1, f32[1,1024]{1,0:T(1,128)} %gain.1, f32[1,1024]{1,0:T(1,128)} %readv.1, s32[64]{0:T(128)} %dil.1, s32[7]{0:T(128)} %order.1), custom_call_target="tpu_custom_call" | custom-call | tf_op jit(solution)/shard_map/pallas_call | solution.py:458
  267.0 1.3 copy.9

commit v4 on v3

--- a/solution.py
+++ b/solution.py
@@ -82,7 +82,7 @@
 def kernel(
     series, wqkv, wout, gain, readv, dil, order, out,
     stage, ser_rx, h, grs, wq, wo, relay_q, relay_o, near_rx, far_rx, near_own, far_own, qs, heads, totals, out_rx,
-    ser_send, ser_recv, gr_send, gr_recv, root_send, relay_recv, swap_send, rl_send, w_recv, fw_send, fw_recv,
+    ser_send, ser_recv, gr_send, gr_recv, root_send, relay_recv, swap_send, rl_send, w_recv, fw_send, fw_recv, own_sem,
     near_send, near_recv, far_send, far_recv, out_send, out_recv, credit,
 ):
     sec = lax.axis_index("section")
@@ -265,9 +265,17 @@
                 landed(part_q(step, k), relay_recv.at[step, k, 0])
                 landed(part_o(step, k), relay_recv.at[step, k, 1])
             for j in range(4):
-                relay_copy_q(step, j).start()
+
+                @pl.when(neighbours[j] != step)
+                def _(j=j):
+                    relay_copy_q(step, j).start()
+
             for j in range(4):
-                relay_copy_o(step, j).start()
+
+                @pl.when(neighbours[j] != step)
+                def _(j=j):
+                    relay_copy_o(step, j).start()
+
 
             @pl.when(step + 1 < LAYERS)
             def _():
@@ -276,8 +284,12 @@
         @pl.loop(0, LAYERS)
         def _(step):
             for j in range(4):
-                relay_copy_q(step, j).wait_send()
-                relay_copy_o(step, j).wait_send()
+
+                @pl.when(neighbours[j] != step)
+                def _(j=j):
+                    relay_copy_q(step, j).wait_send()
+                    relay_copy_o(step, j).wait_send()
+
             for i in range(3):
                 for one in part_copies(step, i):
                     one.wait_send()
@@ -292,11 +304,30 @@
         half = wo.at[slot, pl.ds(pl.multiple_of(c * 256, 256), 256)]
         return copy(half, half, fw_send.at[slot, 1], fw_recv.at[slot, 1], sibling)
 
-    def landed_half(step, which):
-        slot = step % SLOTS
-        landed((wq.at[slot, pl.ds(0, 512)], wo.at[slot, pl.ds(0, 256)])[which], fw_recv.at[slot, which])
+    def own_copy(which):
+        src, dst = ((wqkv, wq), (wout, wo))[which]
+        return pltpu.make_async_copy(src.at[0], dst.at[sec % SLOTS], own_sem.at[which])
+
+    def landed_all(step, which):
+        @pl.when(step == sec)
+        def _():
+            own_copy(which).wait()
+
+        @pl.when(step != sec)
+        def _():
+            (half_copy_q, half_copy_o)[which](step).wait_recv()
 
     def share_half(step):
+        @pl.when(step == sec)
+        def _():
+            own_copy(0).start()
+            own_copy(1).start()
+
+        @pl.when(step != sec)
+        def _():
+            share_half_of(step)
+
+    def share_half_of(step):
         slot = step % SLOTS
         for q in range(4):
             e = 4 * c + q
@@ -323,7 +354,7 @@
         def _():
             root_start()
 
-        landed_half(step, 0)
+        landed_all(step, 0)
         landed(grs.at[step, 0], gr_recv.at[step, 0])
         hidden = h[...].astype(F32)
         scale = lax.rsqrt(jnp.mean(hidden * hidden, axis=-1, keepdims=True) + EPSILON)
@@ -360,10 +391,6 @@
             near_copy(step, kv).wait_recv()
             near_pass(step, kv).start()
 
-        @pl.when(step + 1 < LAYERS)
-        def _():
-            share_half(step + 1)
-
         oldest = (col > row) & (shard >= 2)
         middle = (col >= 0) & (shard >= 1)
         begun = []
@@ -378,13 +405,17 @@
                     ),
                 )
             )
+        @pl.when(step + 1 < LAYERS)
+        def _():
+            share_half(step + 1)
+
         for kv in range(2):
             near_pass(step, kv).wait_recv()
         for head in range(HEADS):
             k = slice(head * HD, (head + 1) * HD)
             last = (near_rx[step, 1, 0, :, k], near_rx[step, 1, 1, :, k], oldest)
             heads[:, k] = weighted(attend(qs[:, k], (last,), begun[head]))
-        landed_half(step, 1)
+        landed_all(step, 1)
         landed(grs.at[step, 1], gr_recv.at[step, 1])
         updated = (h[...].astype(F32) + dot(heads[...], wo[slot])).astype(BF)
         h[...] = updated
@@ -397,8 +428,11 @@
             near_copy(step, kv).wait_send()
             near_pass(step, kv).wait_send()
         far_copy(step).wait_send()
-        half_copy_q(step).wait_send()
-        half_copy_o(step).wait_send()
+        @pl.when(step != sec)
+        def _():
+            half_copy_q(step).wait_send()
+            half_copy_o(step).wait_send()
+
 
         @pl.when(step + SLOTS < LAYERS)
         def _():
@@ -481,7 +515,7 @@
             dma((8, 2)), dma((LAYERS, 2)),
             dma((8, 2)), dma((LAYERS, 4, 2)), dma((LAYERS, 3, 2)),
             dma((LAYERS, 4, 2)), dma((SLOTS, 4, 2)),
-            dma((SLOTS, 2)), dma((SLOTS, 2)),
+            dma((SLOTS, 2)), dma((SLOTS, 2)), dma((2,)),
             dma((2, 2)), dma((LAYERS, 2, 2)),
             dma((1,)), dma((LAYERS,)),
             dma((LAYERS,)), dma((MICRO,)),

time: 272 us -> 266 us (0.978); the launches traced: 268 us -> 266 us
  Pallas kernels: 267 us -> 264 us
where the time goes in v4:
time: 266 us
  Pallas kernels  264 us (99%)
    pallas_call x1, Pallas kernels, local(): pl.pallas_call(kernel, out_shape=jax.ShapeDtypeStruct((MICRO, 1, 8), F32)...  264 us

profile of v4, /device:TPU:1, one launch (start us, length us, event | category | flops | bytes accessed | tf_op | source)
XLA Modules:
  0.0 265.6 jit_solution(1458670581401050423)
XLA Ops:
  0.0 264.4 %shard_map.73 = f32[7,1,8]{2,1,0:T(1,128)} custom-call(bf16[7,64,128]{2,1,0:T(8,128)(2,1)} %bitcast.1, bf16[1,1024,1536]{2,1,0:T(8,128)(2,1)} %wqkv.1, bf16[1,512,1024]{2,1,0:T(8,128)(2,1)} %wout.1, f32[1,1024]{1,0:T(1,128)} %gain.1, f32[1,1024]{1,0:T(1,128)} %readv.1, s32[64]{0:T(128)} %dil.1, s32[7]{0:T(128)} %order.1), custom_call_target="tpu_custom_call" | custom-call | tf_op jit(solution)/shard_map/pallas_call | solution.py:492
  264.4 1.3 copy.9
